TPU v7x, 32 devices: a whole 2x2x4 slice. The times are simulated.
32 devices in a mesh: lat: 4 (over y, core), lon: 8 (over z, x).
Axes of the slice: x: 2, y: 2, z: 4, core: 2. Of those that a mesh axis runs over, the one named last changes fastest.
Arguments:
- grid_fields: bfloat16 [24, 64, 1024], P(None, 'lat', 'lon'), may hold values from -6 to 6
- obs_values: bfloat16 [32, 32, 16, 128], P(('lat', 'lon')), may hold values from -6 to 6
- obs_count: int32 [32, 32], P(('lat', 'lon')), may hold values from 0 to 16, as said below
- obs_cell: int32 [32, 32, 16], P(('lat', 'lon')), may hold values from 0 to 2047
- obs_valid: int32 [32, 32, 16], P(('lat', 'lon')), may hold values 0 or 1
- obs_dist2: float32 [32, 32, 16], P(('lat', 'lon')), may hold values from 0.01 to 4
- field_weight: bfloat16 [24, 128], replicated, may hold values from -1.25 to 1.25
- obs_weight: bfloat16 [128, 128], replicated, may hold values from -0.5 to 0.5
- conv_kernel: bfloat16 [2, 5, 5, 128, 128], replicated, may hold values from -0.109375 to 0.109375
- cotangent: bfloat16 [64, 1024, 128], P('lat', 'lon'), may hold values from -6 to 6
Outputs:
- encoded: bfloat16 [64, 1024, 128], P('lat', 'lon')
- kernel_grad: float32 [2, 5, 5, 128, 128], replicated
- obs_weight_grad: float32 [128, 128], replicated
- field_weight_grad: float32 [24, 128], replicated
Inputs may be any that keep to these rules, and one draw needn't show every extreme that they name: Rows from slot index obs_count onwards are padding. Every tile receives a full slot of 16 rows from some sending device.
All inputs are finite; a program needn't handle non-finite values. No bound on the sum of `obs_valid` on one device may be relied on, other than what follows from the above.
Results may differ from a plain program's by a relative error of at most 0.01.
Values may be sent and summed in bfloat16 or wider, within the bound.
A program may use at most 128 MiB of HBM per device.

v0:
```python
import functools

import jax
import jax.numpy as jnp
from jax import lax
from jax.experimental import pallas as pl
from jax.experimental.pallas import tpu as pltpu
from jax.sharding import PartitionSpec as P

BF16 = jnp.bfloat16
F32 = jnp.float32
MESH = pl.DeviceIdType.MESH
TAPS = 5
SIDE = 16
ROOT = 0.7978845608028654


def gelu_pair(x):
    cubic = 0.044715 * x * x
    bend = jnp.tanh(ROOT * x * (1.0 + cubic))
    half = 0.5 * (1.0 + bend)
    slope = half + 0.5 * x * (1.0 - bend * bend) * (ROOT * (1.0 + 3.0 * cubic))
    return x * half, slope


def stage_plan(lat_parts, lon_parts, lat_first):
    lat = [("lat", 2, 1), ("lat", lat_parts // 2, 2)] if lat_parts % 2 == 0 else [("lat", lat_parts, 1)]
    lon = [("lon", 2, 1), ("lon", lon_parts // 2, 2)] if lon_parts % 2 == 0 else [("lon", lon_parts, 1)]
    if lat_first:
        plan = lat + lon
    else:
        plan = lat[:1] + lon[:1] + lat[1:] + lon[1:]
    return [stage for stage in plan if stage[1] > 1]


class Group:
    def __init__(self, stage, lat, lon):
        self.axis, self.size, self.stride = stage
        self.lat, self.lon = lat, lon
        pos = lat if self.axis == "lat" else lon
        self.rank = lax.rem(pos // self.stride, self.size)
        self.pos = pos

    def rank_at(self, dist):
        return lax.rem(self.rank + dist, self.size)

    def device(self, rank):
        pos = self.pos + (rank - self.rank) * self.stride
        return (pos, self.lon) if self.axis == "lat" else (self.lat, pos)


def kernel(
    lat_parts, lon_parts,
    fields_ref, values_ref, count_ref, cell_ref, valid_ref, dist_ref,
    field_w_ref, obs_w_ref, conv_ref, cot_ref,
    enc_ref, kgrad_ref, small_ref,
    header, vrecv, hrecv, featx, wcat, wbuf, pad_g2, pad_a1, pad_a2, pad_g1,
    left, right, turned, shifted, shifted_side, back2, x_keep, slope1, slope2,
    kacc, part, final, inbox, small, small_in,
    a2a_send, a2a_recv, own_sem, halo_send, halo_recv,
    rs_send, rs_recv, ag_send, ag_recv, sm_send, sm_recv,
):
    lat = lax.axis_index("lat")
    lon = lax.axis_index("lon")
    parts = lat_parts * lon_parts
    me = lat * lon_parts + lon
    rows, cols, channels = cot_ref.shape
    capacity = values_ref.shape[2]
    side = slice(cols, cols + SIDE)
    wide = cols + SIDE
    tile_count = part.shape[1]

    def device_at(dist):
        peer = lax.rem(me + dist, parts)
        return peer, (peer // lon_parts, lax.rem(peer, lon_parts))

    barrier = pltpu.get_barrier_semaphore()

    @pl.loop(1, parts)
    def _(dist):
        pl.semaphore_signal(barrier, inc=1, device_id=device_at(dist)[1], device_id_type=MESH)

    ii = lax.broadcasted_iota(jnp.int32, (parts, parts), 0)
    jj = lax.broadcasted_iota(jnp.int32, (parts, parts), 1)
    counts = jnp.sum(
        jnp.where(ii == jj, jnp.broadcast_to(count_ref[...], (parts, parts)), 0).astype(F32),
        axis=1, keepdims=True,
    )
    slot = lax.broadcasted_iota(jnp.int32, (parts, capacity), 1).astype(F32)
    used = (valid_ref[0] == 1) & (slot < counts)
    weight = jnp.where(used, jnp.exp(-0.5 * dist_ref[0]), 0.0).astype(BF16).astype(F32)
    header[...] = jnp.zeros_like(header)
    header[:, 0, 0:capacity] = weight
    header[:, 1, 0:capacity] = cell_ref[0].astype(F32)

    def clear_edges(pad, k):
        zero = jnp.zeros((2, wide, channels), BF16)
        zero_side = jnp.zeros((2, SIDE, channels), BF16)

        @pl.when(lat == 0)
        def _():
            pad[0:2] = zero
            left[k, 0:2] = zero_side
            right[k, 0:2] = zero_side

        @pl.when(lat == lat_parts - 1)
        def _():
            pad[rows + 2 : rows + 4] = zero
            left[k, rows + 2 : rows + 4] = zero_side
            right[k, rows + 2 : rows + 4] = zero_side

    def halo_copies(pad, k):
        up, down = lat - 1, lat + 1
        west = lax.rem(lon + lon_parts - 1, lon_parts)
        east = lax.rem(lon + 1, lon_parts)
        first, last = slice(2, 4), slice(rows, rows + 2)
        above, below = slice(0, 2), slice(rows + 2, rows + 4)
        middle = slice(2, rows + 2)
        lo, hi, full = slice(0, SIDE), slice(cols - SIDE, cols), slice(0, cols)
        has_up, has_down = lat > 0, lat < lat_parts - 1
        table = [
            (pad.at[first, full], pad.at[below, full], (up, lon), has_up, has_down),
            (pad.at[last, full], pad.at[above, full], (down, lon), has_down, has_up),
            (pad.at[middle, lo], right.at[k, middle], (lat, west), None, None),
            (pad.at[middle, hi], left.at[k, middle], (lat, east), None, None),
            (pad.at[first, lo], right.at[k, below], (up, west), has_up, has_down),
            (pad.at[first, hi], left.at[k, below], (up, east), has_up, has_down),
            (pad.at[last, lo], right.at[k, above], (down, west), has_down, has_up),
            (pad.at[last, hi], left.at[k, above], (down, east), has_down, has_up),
        ]
        out = []
        for n, (src, dst, dev, can_send, can_recv) in enumerate(table):
            copy = pltpu.make_async_remote_copy(
                src_ref=src, dst_ref=dst, send_sem=halo_send.at[k, n], recv_sem=halo_recv.at[k, n],
                device_id=dev, device_id_type=MESH,
            )
            out.append((copy, can_send, can_recv))
        return out

    def guarded(cond, act):
        if cond is None:
            act()
        else:
            pl.when(cond)(act)

    def halo_start(copies):
        for copy, can_send, _ in copies:
            guarded(can_send, copy.start)

    def halo_finish(copies, pad, k):
        for copy, _, can_recv in copies:
            guarded(can_recv, copy.wait_recv)
        at = lax.broadcasted_iota(jnp.int32, (SIDE, channels), 0)

        @pl.loop(0, rows + 4)
        def _(h):
            r = right[k, h].astype(F32)
            l = left[k, h].astype(F32)
            pad[h, side] = jnp.where(at < 2, r, jnp.where(at >= SIDE - 2, l, 0.0)).astype(BF16)

    def halo_drain(copies):
        for copy, can_send, _ in copies:
            guarded(can_send, copy.wait_send)

    def place_weights(layer, turn):
        for p in range(TAPS):
            for q in range(TAPS):
                if turn:
                    block = conv_ref[layer, TAPS - 1 - p, TAPS - 1 - q].T
                else:
                    block = conv_ref[layer, p, q]
                wbuf[p * channels : (p + 1) * channels, q * channels : (q + 1) * channels] = block

    group = 4 if rows % 4 == 0 else 1

    def conv(pad, finish):
        @pl.loop(0, rows // group)
        def _(b):
            lhs = jnp.concatenate(
                [pad[pl.ds(b * group + p, group)].reshape(group * wide, channels) for p in range(TAPS)],
                axis=1,
            )
            prod = jnp.dot(lhs, wbuf[...], preferred_element_type=F32)
            for r in range(group):
                total = None
                for q in range(TAPS):
                    piece = prod[r * wide : (r + 1) * wide, q * channels : (q + 1) * channels]
                    shift = (2 - q) % wide
                    if shift:
                        piece = pltpu.roll(piece, shift, 0)
                    piece = piece[:cols]
                    total = piece if total is None else total + piece
                finish(b * group + r, total)

    def shift_grad(pad):
        @pl.loop(0, rows)
        def _(h):
            ext = jnp.concatenate(
                [pad[h + 2, 0:cols].astype(F32), jnp.zeros((SIDE, channels), F32)], axis=0
            )
            for q in range(TAPS):
                shift = (q - 2) % wide
                moved = (pltpu.roll(ext, shift, 0) if shift else ext).astype(BF16)
                lanes = slice(q * channels, (q + 1) * channels)
                shifted[h, :, lanes] = moved[:cols]
                shifted_side[h, :, lanes] = moved[cols:]

    def turn_act(pad):
        @pl.loop(0, rows + 4)
        def _(h):
            turned[h] = pad[h, 0:cols].T

    def kernel_terms(pad, slot_of):
        side_lhs = jnp.concatenate(
            [pad[p : p + rows, side].reshape(rows * SIDE, channels).T for p in range(TAPS)], axis=0
        )
        kacc[...] = jnp.dot(
            side_lhs, shifted_side[...].reshape(rows * SIDE, TAPS * channels),
            preferred_element_type=F32,
        )

        @pl.loop(0, rows // group)
        def _(b):
            lhs = jnp.concatenate(
                [
                    jnp.concatenate([turned[b * group + p + r] for r in range(group)], axis=1)
                    for p in range(TAPS)
                ],
                axis=0,
            )
            rhs = shifted[pl.ds(b * group, group)].reshape(group * cols, TAPS * channels)
            kacc[...] += jnp.dot(lhs, rhs, preferred_element_type=F32)

        per = channels // 16
        for p in range(TAPS):
            for q in range(TAPS):
                block = kacc[p * channels : (p + 1) * channels, q * channels : (q + 1) * channels]
                n = (p * TAPS + q) * per
                part[slot_of, n : n + per] = block.astype(BF16).reshape(per, 16, channels)
        used_tiles = TAPS * TAPS * per
        if used_tiles < tile_count:
            part[slot_of, used_tiles:] = jnp.zeros(
                (tile_count - used_tiles, 16, channels), BF16
            )

    def sum_steps(slot_of, plan):
        groups = [Group(stage, lat, lon) for stage in plan]
        pending = []
        base = jnp.int32(0)
        length = tile_count
        box = 0
        nsem = 0
        bases = []
        for g in groups:
            share = length // g.size
            sent = []
            for dist in range(1, g.size):
                copy = pltpu.make_async_remote_copy(
                    src_ref=part.at[slot_of, pl.ds(base + g.rank_at(dist) * share, share)],
                    dst_ref=inbox.at[slot_of, pl.ds(box + (dist - 1) * share, share)],
                    send_sem=rs_send.at[slot_of, nsem], recv_sem=rs_recv.at[slot_of, nsem],
                    device_id=g.device(g.rank_at(dist)), device_id_type=MESH,
                )
                copy.start()
                sent.append(copy)
                nsem += 1
            pending += sent
            yield
            for copy in sent:
                copy.wait_recv()
            mine = base + g.rank * share
            total = part[slot_of, pl.ds(mine, share)].astype(F32)
            for dist in range(1, g.size):
                at = box + (dist - 1) * share
                total = total + inbox[slot_of, at : at + share].astype(F32)
            part[slot_of, pl.ds(mine, share)] = total.astype(BF16)
            box += (g.size - 1) * share
            bases.append(base)
            base, length = mine, share
        final[slot_of, pl.ds(base, length)] = part[slot_of, pl.ds(base, length)]
        nsem = 0
        for g, low in zip(reversed(groups), reversed(bases)):
            sent, got = [], []
            for dist in range(1, g.size):
                copy = pltpu.make_async_remote_copy(
                    src_ref=final.at[slot_of, pl.ds(base, length)],
                    dst_ref=final.at[slot_of, pl.ds(base, length)],
                    send_sem=ag_send.at[slot_of, nsem], recv_sem=ag_recv.at[slot_of, nsem],
                    device_id=g.device(g.rank_at(dist)), device_id_type=MESH,
                )
                copy.start()
                sent.append(copy)
                here = final.at[slot_of, pl.ds(low + g.rank_at(g.size - dist) * length, length)]
                got.append(
                    pltpu.make_async_remote_copy(
                        src_ref=here, dst_ref=here,
                        send_sem=ag_send.at[slot_of, nsem], recv_sem=ag_recv.at[slot_of, nsem],
                        device_id=g.device(g.rank_at(dist)), device_id_type=MESH,
                    )
                )
                nsem += 1
            pending += sent
            yield
            for copy in got:
                copy.wait_recv()
            base, length = low, length * g.size
        for copy in pending:
            copy.wait_send()
        kgrad_ref[slot_of] = final[slot_of]

    def small_steps(plan):
        nsem = 0
        pending = []
        for n, stage in enumerate(plan):
            g = Group(stage, lat, lon)
            sent = []
            for dist in range(1, g.size):
                copy = pltpu.make_async_remote_copy(
                    src_ref=small.at[n], dst_ref=small_in.at[nsem],
                    send_sem=sm_send.at[nsem], recv_sem=sm_recv.at[nsem],
                    device_id=g.device(g.rank_at(dist)), device_id_type=MESH,
                )
                copy.start()
                sent.append((copy, nsem, dist))
                nsem += 1
            pending += sent
            yield
            for copy, _, _ in sent:
                copy.wait_recv()
            total = jnp.zeros(small.shape[1:], F32)
            mine = small[n].astype(F32)
            for rank in range(g.size):
                term = mine
                for _, box, dist in sent:
                    term = jnp.where(g.rank_at(g.size - dist) == rank, small_in[box].astype(F32), term)
                total = total + term
            small[n + 1] = total.astype(BF16)
        for copy, _, _ in pending:
            copy.wait_send()
        small_ref[...] = small[len(plan)]

    pad_g2[2 : rows + 2, 0:cols] = cot_ref[...]
    for k, pad in enumerate((pad_g2, pad_a1, pad_a2, pad_g1)):
        clear_edges(pad, k)
    place_weights(1, True)
    field_count = fields_ref.shape[0]
    width = values_ref.shape[3]
    featx[width:, :] = jnp.zeros((featx.shape[0] - width, featx.shape[1]), BF16)
    featx[width : width + field_count, :] = fields_ref[...]
    wcat[...] = jnp.zeros_like(wcat)
    wcat[0:width] = obs_w_ref[...]
    wcat[width : width + field_count] = field_w_ref[...]

    pl.semaphore_wait(barrier, parts - 1)

    own = pltpu.make_async_copy(values_ref.at[0, me], vrecv.at[me], own_sem.at[0])
    own.start()
    own_head = pltpu.make_async_copy(header.at[me], hrecv.at[me], own_sem.at[1])
    own_head.start()

    def row_copies(dist):
        peer, dev = device_at(dist)
        return [
            pltpu.make_async_remote_copy(
                src_ref=src, dst_ref=dst, send_sem=a2a_send.at[n, dist], recv_sem=a2a_recv.at[n, dist],
                device_id=dev, device_id_type=MESH,
            )
            for n, (src, dst) in enumerate(
                ((values_ref.at[0, peer], vrecv.at[me]), (header.at[peer], hrecv.at[me]))
            )
        ]

    @pl.loop(1, parts)
    def _(dist):
        for copy in row_copies(dist):
            copy.start()

    halo_g2 = halo_copies(pad_g2, 0)
    halo_start(halo_g2)
    halo_finish(halo_g2, pad_g2, 0)

    def keep_back(h, total):
        back2[h] = total

    conv(pad_g2, keep_back)
    place_weights(0, False)

    own.wait()
    own_head.wait()

    @pl.loop(1, parts)
    def _(dist):
        sender = lax.rem(me + parts - dist, parts)
        for n, dst in enumerate((vrecv.at[sender], hrecv.at[sender])):
            pltpu.make_async_remote_copy(
                src_ref=dst, dst_ref=dst, send_sem=a2a_send.at[n, dist], recv_sem=a2a_recv.at[n, dist],
                device_id=device_at(dist)[1], device_id_type=MESH,
            ).wait_recv()

    count = parts * capacity
    lane = lax.broadcasted_iota(jnp.int32, (count, 128), 1)
    pick = lane == lax.rem(lax.broadcasted_iota(jnp.int32, (count, 128), 0), capacity)

    def column(n):
        spread = jnp.broadcast_to(hrecv[:, n : n + 1, :], (parts, capacity, 128)).reshape(count, 128)
        return jnp.sum(jnp.where(pick, spread, 0.0), axis=1, keepdims=True)

    w_col, cell_col = column(0), column(1)
    values_t = jnp.concatenate(
        [vrecv[...].reshape(count, width).T, jnp.ones((16, count), BF16)], axis=0
    )
    block = 512 if (rows * cols) % 512 == 0 else cols

    @pl.loop(0, rows * cols // block)
    def _(b):
        start = pl.multiple_of(b * block, block)
        ids = (start + lax.broadcasted_iota(jnp.int32, (count, block), 1)).astype(F32)
        spread = jnp.where(ids == cell_col, w_col, 0.0).astype(BF16)
        sums = jnp.dot(values_t, spread, preferred_element_type=F32)
        dens = sums[width : width + 1]
        featx[0:width, pl.ds(start, block)] = (sums[0:width] / (1.0 + dens)).astype(BF16)

    @pl.loop(0, rows)
    def _(h):
        start = pl.multiple_of(h * cols, cols)
        feats = featx[:, pl.ds(start, cols)].T
        x = jnp.dot(feats, wcat[...], preferred_element_type=F32).astype(BF16).astype(F32)
        act, slope = gelu_pair(x)
        x_keep[h] = x
        slope1[h] = slope
        pad_a1[h + 2, 0:cols] = act.astype(BF16)

    halo_a1 = halo_copies(pad_a1, 1)
    halo_start(halo_a1)
    halo_finish(halo_a1, pad_a1, 1)

    def first_layer(h, total):
        x = (x_keep[h] + total).astype(BF16).astype(F32)
        act, slope = gelu_pair(x)
        x_keep[h] = x
        pad_a2[h + 2, 0:cols] = act.astype(BF16)
        g = cot_ref[h].astype(F32) + slope * back2[h]
        pad_g1[h + 2, 0:cols] = g.astype(BF16)

    conv(pad_a1, first_layer)
    halo_a2 = halo_copies(pad_a2, 2)
    halo_start(halo_a2)
    halo_g1 = halo_copies(pad_g1, 3)
    halo_start(halo_g1)

    turn_act(pad_a1)
    shift_grad(pad_g1)
    kernel_terms(pad_a1, 0)
    sum_a = sum_steps(0, stage_plan(lat_parts, lon_parts, True))
    next(sum_a)

    halo_finish(halo_a2, pad_a2, 2)
    turn_act(pad_a2)
    shift_grad(pad_g2)
    next(sum_a, None)
    kernel_terms(pad_a2, 1)
    sum_b = sum_steps(1, stage_plan(lat_parts, lon_parts, False))
    next(sum_b)
    next(sum_a, None)

    place_weights(0, True)
    halo_finish(halo_g1, pad_g1, 3)

    def last_grad(h, total):
        g = pad_g1[h + 2, 0:cols].astype(F32) + slope1[h] * total
        back2[h] = g

    conv(pad_g1, last_grad)
    next(sum_b, None)
    grads = jnp.dot(
        featx[...], back2[...].astype(BF16).reshape(rows * cols, channels), preferred_element_type=F32
    )
    small[0] = grads[0 : small.shape[1]].astype(BF16)
    sum_c = small_steps(stage_plan(lat_parts, lon_parts, True))
    next(sum_c)
    next(sum_a, None)
    next(sum_b, None)

    place_weights(1, False)

    def last_layer(h, total):
        enc_ref[h] = (x_keep[h] + total).astype(BF16)

    conv(pad_a2, last_layer)

    live = [sum_c, sum_a, sum_b]
    while live:
        live = [s for s in live if next(s, "end") != "end"]

    for copies in (halo_g2, halo_a1, halo_a2, halo_g1):
        halo_drain(copies)

    @pl.loop(1, parts)
    def _(dist):
        for copy in row_copies(dist):
            copy.wait_send()


def per_device(
    grid_fields, obs_values, obs_count, obs_cell, obs_valid, obs_dist2,
    field_weight, obs_weight, conv_kernel, cotangent,
):
    rows, cols, channels = cotangent.shape
    lat_parts = lax.axis_size("lat")
    lon_parts = lax.axis_size("lon")
    parts = lat_parts * lon_parts
    fields = grid_fields.shape[0]
    width = obs_values.shape[3]
    capacity = obs_values.shape[2]
    wide = cols + SIDE
    tiles = TAPS * TAPS * channels // 16
    tiles = -(-tiles // parts) * parts
    plan = stage_plan(lat_parts, lon_parts, True)
    hops = sum(stage[1] - 1 for stage in plan)
    deep = -(-(width + fields) // 128) * 128
    small_rows = -(-(width + fields) // 16) * 16
    vmem = pl.BlockSpec(memory_space=pltpu.VMEM)
    pads = [pltpu.VMEM((rows + 4, wide, channels), BF16)] * 4
    encoded, kgrad, small = pl.pallas_call(
        functools.partial(kernel, lat_parts, lon_parts),
        out_shape=(
            jax.ShapeDtypeStruct((rows, cols, channels), BF16),
            jax.ShapeDtypeStruct((2, tiles, 16, channels), BF16),
            jax.ShapeDtypeStruct((small_rows, channels), BF16),
        ),
        in_specs=[vmem] * 10,
        out_specs=(vmem, vmem, vmem),
        scratch_shapes=[
            pltpu.VMEM((parts, 2, 128), F32),
            pltpu.VMEM((parts, capacity, width), BF16),
            pltpu.VMEM((parts, 2, 128), F32),
            pltpu.VMEM((deep, rows * cols), BF16),
            pltpu.VMEM((deep, channels), BF16),
            pltpu.VMEM((TAPS * channels, TAPS * channels), BF16),
            *pads,
            pltpu.VMEM((4, rows + 4, SIDE, channels), BF16),
            pltpu.VMEM((4, rows + 4, SIDE, channels), BF16),
            pltpu.VMEM((rows + 4, channels, cols), BF16),
            pltpu.VMEM((rows, cols, TAPS * channels), BF16),
            pltpu.VMEM((rows, SIDE, TAPS * channels), BF16),
            pltpu.VMEM((rows, cols, channels), F32),
            pltpu.VMEM((rows, cols, channels), F32),
            pltpu.VMEM((rows, cols, channels), F32),
            pltpu.VMEM((rows, cols, channels), F32),
            pltpu.VMEM((TAPS * channels, TAPS * channels), F32),
            pltpu.VMEM((2, tiles, 16, channels), BF16),
            pltpu.VMEM((2, tiles, 16, channels), BF16),
            pltpu.VMEM((2, tiles, 16, channels), BF16),
            pltpu.VMEM((len(plan) + 1, small_rows, channels), BF16),
            pltpu.VMEM((hops, small_rows, channels), BF16),
            pltpu.SemaphoreType.DMA((2, parts)),
            pltpu.SemaphoreType.DMA((2, parts)),
            pltpu.SemaphoreType.DMA((2,)),
            pltpu.SemaphoreType.DMA((4, 8)),
            pltpu.SemaphoreType.DMA((4, 8)),
            pltpu.SemaphoreType.DMA((2, hops)),
            pltpu.SemaphoreType.DMA((2, hops)),
            pltpu.SemaphoreType.DMA((2, hops)),
            pltpu.SemaphoreType.DMA((2, hops)),
            pltpu.SemaphoreType.DMA((hops,)),
            pltpu.SemaphoreType.DMA((hops,)),
        ],
        compiler_params=pltpu.CompilerParams(
            collective_id=0, has_side_effects=True, vmem_limit_bytes=56 * 1024 * 1024
        ),
        name="encoder",
    )(
        grid_fields.reshape(fields, rows * cols), obs_values, obs_count, obs_cell, obs_valid,
        obs_dist2, field_weight, obs_weight, conv_kernel, cotangent,
    )
    scale = 1.0 / (rows * lat_parts * cols * lon_parts) ** 0.5
    used = TAPS * TAPS * channels // 16
    kernel_grad = scale * kgrad[:, :used].astype(F32).reshape(2, TAPS, TAPS, channels, channels)
    small = scale * small.astype(F32)
    return encoded, kernel_grad, small[:width], small[width : width + fields]


def solution(mesh):
    return jax.shard_map(
        per_device,
        mesh=mesh,
        in_specs=(
            P(None, "lat", "lon"),
            P(("lat", "lon"), None, None, None),
            P(("lat", "lon"), None),
            P(("lat", "lon"), None, None),
            P(("lat", "lon"), None, None),
            P(("lat", "lon"), None, None),
            P(),
            P(),
            P(),
            P("lat", "lon", None),
        ),
        out_specs=(P("lat", "lon", None), P(), P(), P()),
        check_vma=False,
    )
```

profile of v0, /device:TPU:0, one launch (start us, length us, event | category | flops | bytes accessed | tf_op | source)
XLA Modules:
  0.0 101.8 jit_solution(3321929258587787125)
XLA Ops:
  0.6 1.6 %copy.19 = bf16[3,8,16,128]{3,1,2,0:T(8,128)(2,1)} copy(bf16[3,8,16,128]{3,2,1,0:T(8,128)(2,1)} %bitcast.7) | data formatting | bytes 196608
  2.2 1.4 %copy.14.cell_ref = s32[1,32,16]{2,1,0:T(8,128)} copy(s32[1,32,16]{1,2,0:T(8,128)} %param.13) | data formatting | bytes 4096 | tf_op args[3]
  3.6 1.4 %copy.15.valid_ref = s32[1,32,16]{2,1,0:T(8,128)} copy(s32[1,32,16]{1,2,0:T(8,128)} %param.14) | data formatting | bytes 4096 | tf_op args[4]
  4.9 1.4 %copy.16.dist_ref = f32[1,32,16]{2,1,0:T(8,128)} copy(f32[1,32,16]{1,2,0:T(8,128)} %param.15) | data formatting | bytes 4096 | tf_op args[5]
  6.3 90.0 %encoder.1 = (bf16[16,128,128]{2,1,0:T(8,128)(2,1)}, bf16[2,224,16,128]{3,2,1,0:T(8,128)(2,1)}, bf16[160,128]{1,0:T(8,128)(2,1)}) custom-call(bf16[24,2048]{1,0:T(8,128)(2,1)} %bitcast.6, bf16[1,32,16,128]{3,2,1,0:T(8,128)(2,1)} %values_ref.1, s32[1,32]{1,0:T(1,128)} %count_ref.1, s32[1,32,16]{2,1,0:T(8,128)} %copy.14.cell_ref, ...), custom_call_target="tpu_custom_call" | custom-call | tf_op jit(solution)/shard_map/encoder/pallas_call | solution.py:524
  96.3 0.0 copy-start.1
  96.3 0.0 copy-start
  96.3 3.5 %convert_multiply_fusion = f32[2,200,16,128]{3,2,1,0:T(8,128)} fusion(bf16[2,224,16,128]{3,2,1,0:T(8,128)(2,1)} %get-tuple-element.8), kind=kLoop, calls=%fused_computation | loop fusion | flops 1638400 | bytes 4915200 | tf_op jit(solution)/shard_map/mul | solution.py:578
  99.7 0.0 copy-done.1
  99.8 0.6 slice.12
  100.4 0.6 slice.13
  101.0 0.0 copy-done
  101.0 0.8 copy.21
  (1 shorter events, 0.0 us)
Async XLA Ops:
  96.3 3.5 %copy-start.1 = (bf16[160,128]{1,0:T(8,128)(2,1)S(1)}, bf16[160,128]{1,0:T(8,128)(2,1)}, u32[]{:S(2)}) copy-start(bf16[160,128]{1,0:T(8,128)(2,1)} %get-tuple-element.9) | copy-start | bytes 122884
  96.3 4.7 %copy-start = (bf16[16,128,128]{2,1,0:T(8,128)(2,1)S(1)}, bf16[16,128,128]{2,1,0:T(8,128)(2,1)}, u32[]{:S(2)}) copy-start(bf16[16,128,128]{2,1,0:T(8,128)(2,1)} %get-tuple-element.14) | copy-start | bytes 1572868
where the time goes:
time: 102 us
  Pallas kernels  90 us (88%)
  local copies, waits for them, and re-layouts  7.71 us (8%)
  other arithmetic  3.47 us (3%)
    pallas_call x1, Pallas kernels, per_device(): pl.pallas_call(functools.partial(kernel, lat_parts, lon_parts), out_shape...  90 us
    unnamed x9, local copies, waits for them, and re-layouts  6.48 us
    mul x1, other arithmetic, per_device(): scale * kgrad[:, :used].astype(F32).reshape(2, TAPS, TAPS, channels, chan...  3.46 us

commit v1 on v0

--- a/solution.py
+++ b/solution.py
@@ -1,4 +1,5 @@
 import functools
+import math
 
 import jax
 import jax.numpy as jnp
@@ -55,7 +56,8 @@
     field_w_ref, obs_w_ref, conv_ref, cot_ref,
     enc_ref, kgrad_ref, small_ref,
     header, vrecv, hrecv, featx, wcat, wbuf, pad_g2, pad_a1, pad_a2, pad_g1,
-    left, right, turned, shifted, shifted_side, back2, x_keep, slope1, slope2,
+    left, right, strip_out, strip_in, strip_w, strip_e, strip_z, field_rows,
+    turned, shifted, shifted_side, back2, x_keep, slope1,
     kacc, part, final, inbox, small, small_in,
     a2a_send, a2a_recv, own_sem, halo_send, halo_recv,
     rs_send, rs_recv, ag_send, ag_recv, sm_send, sm_recv,
@@ -80,18 +82,12 @@
     def _(dist):
         pl.semaphore_signal(barrier, inc=1, device_id=device_at(dist)[1], device_id_type=MESH)
 
-    ii = lax.broadcasted_iota(jnp.int32, (parts, parts), 0)
-    jj = lax.broadcasted_iota(jnp.int32, (parts, parts), 1)
-    counts = jnp.sum(
-        jnp.where(ii == jj, jnp.broadcast_to(count_ref[...], (parts, parts)), 0).astype(F32),
-        axis=1, keepdims=True,
-    )
-    slot = lax.broadcasted_iota(jnp.int32, (parts, capacity), 1).astype(F32)
-    used = (valid_ref[0] == 1) & (slot < counts)
+    slot = lax.broadcasted_iota(jnp.int32, (capacity, parts), 0)
+    used = (valid_ref[0] == 1) & (slot < count_ref[...])
     weight = jnp.where(used, jnp.exp(-0.5 * dist_ref[0]), 0.0).astype(BF16).astype(F32)
     header[...] = jnp.zeros_like(header)
-    header[:, 0, 0:capacity] = weight
-    header[:, 1, 0:capacity] = cell_ref[0].astype(F32)
+    header[:, 0, 0:capacity] = weight.T
+    header[:, 1, 0:capacity] = cell_ref[0].astype(F32).T
 
     def clear_edges(pad, k):
         zero = jnp.zeros((2, wide, channels), BF16)
@@ -106,8 +102,8 @@
         @pl.when(lat == lat_parts - 1)
         def _():
             pad[rows + 2 : rows + 4] = zero
-            left[k, rows + 2 : rows + 4] = zero_side
-            right[k, rows + 2 : rows + 4] = zero_side
+            left[k, 2:4] = zero_side
+            right[k, 2:4] = zero_side
 
     def halo_copies(pad, k):
         up, down = lat - 1, lat + 1
@@ -115,18 +111,18 @@
         east = lax.rem(lon + 1, lon_parts)
         first, last = slice(2, 4), slice(rows, rows + 2)
         above, below = slice(0, 2), slice(rows + 2, rows + 4)
-        middle = slice(2, rows + 2)
+        top, bottom = slice(0, 2), slice(2, 4)
         lo, hi, full = slice(0, SIDE), slice(cols - SIDE, cols), slice(0, cols)
         has_up, has_down = lat > 0, lat < lat_parts - 1
         table = [
             (pad.at[first, full], pad.at[below, full], (up, lon), has_up, has_down),
             (pad.at[last, full], pad.at[above, full], (down, lon), has_down, has_up),
-            (pad.at[middle, lo], right.at[k, middle], (lat, west), None, None),
-            (pad.at[middle, hi], left.at[k, middle], (lat, east), None, None),
-            (pad.at[first, lo], right.at[k, below], (up, west), has_up, has_down),
-            (pad.at[first, hi], left.at[k, below], (up, east), has_up, has_down),
-            (pad.at[last, lo], right.at[k, above], (down, west), has_down, has_up),
-            (pad.at[last, hi], left.at[k, above], (down, east), has_down, has_up),
+            (strip_out.at[k, 0], strip_in.at[k, 0], (lat, west), None, None),
+            (strip_out.at[k, 1], strip_in.at[k, 1], (lat, east), None, None),
+            (pad.at[first, lo], right.at[k, bottom], (up, west), has_up, has_down),
+            (pad.at[first, hi], left.at[k, bottom], (up, east), has_up, has_down),
+            (pad.at[last, lo], right.at[k, top], (down, west), has_down, has_up),
+            (pad.at[last, hi], left.at[k, top], (down, east), has_down, has_up),
         ]
         out = []
         for n, (src, dst, dev, can_send, can_recv) in enumerate(table):
@@ -143,44 +139,58 @@
         else:
             pl.when(cond)(act)
 
-    def halo_start(copies):
-        for copy, can_send, _ in copies:
+    def halo_start(copies, pad, k):
+        for copy, can_send, _ in copies[:2]:
+            guarded(can_send, copy.start)
+        for copy, can_send, _ in copies[4:]:
+            guarded(can_send, copy.start)
+        strip_w[...] = pad[2 : rows + 2, 0:SIDE].reshape(rows * SIDE, channels).astype(F32)
+        strip_e[...] = (
+            pad[2 : rows + 2, cols - SIDE : cols].reshape(rows * SIDE, channels).astype(F32)
+        )
+        for j in range(2):
+            strip_out[k, 0, j] = strip_w[pl.ds(j, rows, stride=SIDE)].astype(BF16)
+            strip_out[k, 1, j] = strip_e[pl.ds(SIDE - 2 + j, rows, stride=SIDE)].astype(BF16)
+        for copy, can_send, _ in copies[2:4]:
             guarded(can_send, copy.start)
 
     def halo_finish(copies, pad, k):
         for copy, _, can_recv in copies:
             guarded(can_recv, copy.wait_recv)
-        at = lax.broadcasted_iota(jnp.int32, (SIDE, channels), 0)
-
-        @pl.loop(0, rows + 4)
-        def _(h):
-            r = right[k, h].astype(F32)
-            l = left[k, h].astype(F32)
-            pad[h, side] = jnp.where(at < 2, r, jnp.where(at >= SIDE - 2, l, 0.0)).astype(BF16)
+        for j in range(2):
+            strip_z[pl.ds(j, rows, stride=SIDE)] = strip_in[k, 0, j].astype(F32)
+            strip_z[pl.ds(SIDE - 2 + j, rows, stride=SIDE)] = strip_in[k, 1, j].astype(F32)
+        pad[2 : rows + 2, side] = strip_z[...].astype(BF16).reshape(rows, SIDE, channels)
+        at = lax.broadcasted_iota(jnp.int32, (4, SIDE, channels), 1)
+        corner = jnp.where(
+            at < 2, right[k].astype(F32), jnp.where(at >= SIDE - 2, left[k].astype(F32), 0.0)
+        ).astype(BF16)
+        pad[0:2, side] = corner[0:2]
+        pad[rows + 2 : rows + 4, side] = corner[2:4]
 
     def halo_drain(copies):
         for copy, can_send, _ in copies:
             guarded(can_send, copy.wait_send)
 
     def place_weights(layer, turn):
+        at = 2 * layer + turn
         for p in range(TAPS):
             for q in range(TAPS):
                 if turn:
                     block = conv_ref[layer, TAPS - 1 - p, TAPS - 1 - q].T
                 else:
                     block = conv_ref[layer, p, q]
-                wbuf[p * channels : (p + 1) * channels, q * channels : (q + 1) * channels] = block
+                wbuf[at, p * channels : (p + 1) * channels, q * channels : (q + 1) * channels] = block
 
     group = 4 if rows % 4 == 0 else 1
 
-    def conv(pad, finish):
-        @pl.loop(0, rows // group)
-        def _(b):
+    def conv(pad, at, finish, between=None):
+        def one(b):
             lhs = jnp.concatenate(
                 [pad[pl.ds(b * group + p, group)].reshape(group * wide, channels) for p in range(TAPS)],
                 axis=1,
             )
-            prod = jnp.dot(lhs, wbuf[...], preferred_element_type=F32)
+            prod = jnp.dot(lhs, wbuf[at], preferred_element_type=F32)
             for r in range(group):
                 total = None
                 for q in range(TAPS):
@@ -192,7 +202,14 @@
                     total = piece if total is None else total + piece
                 finish(b * group + r, total)
 
-    def shift_grad(pad):
+        if between is None:
+            pl.loop(0, rows // group)(one)
+        else:
+            for b in range(rows // group):
+                one(b)
+                between()
+
+    def shift_grad(pad, at):
         @pl.loop(0, rows)
         def _(h):
             ext = jnp.concatenate(
@@ -202,25 +219,28 @@
                 shift = (q - 2) % wide
                 moved = (pltpu.roll(ext, shift, 0) if shift else ext).astype(BF16)
                 lanes = slice(q * channels, (q + 1) * channels)
-                shifted[h, :, lanes] = moved[:cols]
-                shifted_side[h, :, lanes] = moved[cols:]
+                shifted[at, h, :, lanes] = moved[:cols]
+                shifted_side[at, h, :, lanes] = moved[cols:]
 
     def turn_act(pad):
-        @pl.loop(0, rows + 4)
+        @pl.loop(2, rows + 2)
         def _(h):
             turned[h] = pad[h, 0:cols].T
 
-    def kernel_terms(pad, slot_of):
+    def turn_halo(pad):
+        for h in (0, 1, rows + 2, rows + 3):
+            turned[h] = pad[h, 0:cols].T
+
+    def kernel_terms(pad, slot_of, between=None):
         side_lhs = jnp.concatenate(
             [pad[p : p + rows, side].reshape(rows * SIDE, channels).T for p in range(TAPS)], axis=0
         )
         kacc[...] = jnp.dot(
-            side_lhs, shifted_side[...].reshape(rows * SIDE, TAPS * channels),
+            side_lhs, shifted_side[slot_of].reshape(rows * SIDE, TAPS * channels),
             preferred_element_type=F32,
         )
 
-        @pl.loop(0, rows // group)
-        def _(b):
+        def one(b):
             lhs = jnp.concatenate(
                 [
                     jnp.concatenate([turned[b * group + p + r] for r in range(group)], axis=1)
@@ -228,9 +248,15 @@
                 ],
                 axis=0,
             )
-            rhs = shifted[pl.ds(b * group, group)].reshape(group * cols, TAPS * channels)
+            rhs = shifted[slot_of, pl.ds(b * group, group)].reshape(group * cols, TAPS * channels)
             kacc[...] += jnp.dot(lhs, rhs, preferred_element_type=F32)
 
+        if between is None:
+            pl.loop(0, rows // group)(one)
+        else:
+            for b in range(rows // group):
+                one(b)
+                between()
         per = channels // 16
         for p in range(TAPS):
             for q in range(TAPS):
@@ -243,12 +269,12 @@
                 (tile_count - used_tiles, 16, channels), BF16
             )
 
-    def sum_steps(slot_of, plan):
+    def sum_steps(slot_of, start, length, stream, plan):
         groups = [Group(stage, lat, lon) for stage in plan]
         pending = []
-        base = jnp.int32(0)
-        length = tile_count
-        box = 0
+        base = start
+        box = start
+        whole = slice(start, start + length)
         nsem = 0
         bases = []
         for g in groups:
@@ -258,7 +284,7 @@
                 copy = pltpu.make_async_remote_copy(
                     src_ref=part.at[slot_of, pl.ds(base + g.rank_at(dist) * share, share)],
                     dst_ref=inbox.at[slot_of, pl.ds(box + (dist - 1) * share, share)],
-                    send_sem=rs_send.at[slot_of, nsem], recv_sem=rs_recv.at[slot_of, nsem],
+                    send_sem=rs_send.at[stream, nsem], recv_sem=rs_recv.at[stream, nsem],
                     device_id=g.device(g.rank_at(dist)), device_id_type=MESH,
                 )
                 copy.start()
@@ -285,7 +311,7 @@
                 copy = pltpu.make_async_remote_copy(
                     src_ref=final.at[slot_of, pl.ds(base, length)],
                     dst_ref=final.at[slot_of, pl.ds(base, length)],
-                    send_sem=ag_send.at[slot_of, nsem], recv_sem=ag_recv.at[slot_of, nsem],
+                    send_sem=ag_send.at[stream, nsem], recv_sem=ag_recv.at[stream, nsem],
                     device_id=g.device(g.rank_at(dist)), device_id_type=MESH,
                 )
                 copy.start()
@@ -294,7 +320,7 @@
                 got.append(
                     pltpu.make_async_remote_copy(
                         src_ref=here, dst_ref=here,
-                        send_sem=ag_send.at[slot_of, nsem], recv_sem=ag_recv.at[slot_of, nsem],
+                        send_sem=ag_send.at[stream, nsem], recv_sem=ag_recv.at[stream, nsem],
                         device_id=g.device(g.rank_at(dist)), device_id_type=MESH,
                     )
                 )
@@ -306,7 +332,7 @@
             base, length = low, length * g.size
         for copy in pending:
             copy.wait_send()
-        kgrad_ref[slot_of] = final[slot_of]
+        kgrad_ref[slot_of, whole] = final[slot_of, whole]
 
     def small_steps(plan):
         nsem = 0
@@ -342,11 +368,16 @@
     pad_g2[2 : rows + 2, 0:cols] = cot_ref[...]
     for k, pad in enumerate((pad_g2, pad_a1, pad_a2, pad_g1)):
         clear_edges(pad, k)
+    strip_z[...] = jnp.zeros_like(strip_z)
     place_weights(1, True)
     field_count = fields_ref.shape[0]
     width = values_ref.shape[3]
     featx[width:, :] = jnp.zeros((featx.shape[0] - width, featx.shape[1]), BF16)
-    featx[width : width + field_count, :] = fields_ref[...]
+    field_rows[...] = fields_ref[...].astype(F32).reshape(field_count * rows, cols)
+    for h in range(rows):
+        featx[width : width + field_count, h * cols : (h + 1) * cols] = field_rows[
+            pl.ds(h, field_count, stride=rows)
+        ].astype(BF16)
     wcat[...] = jnp.zeros_like(wcat)
     wcat[0:width] = obs_w_ref[...]
     wcat[width : width + field_count] = field_w_ref[...]
@@ -376,14 +407,15 @@
             copy.start()
 
     halo_g2 = halo_copies(pad_g2, 0)
-    halo_start(halo_g2)
+    halo_start(halo_g2, pad_g2, 0)
+    shift_grad(pad_g2, 1)
+    place_weights(0, False)
     halo_finish(halo_g2, pad_g2, 0)
 
     def keep_back(h, total):
         back2[h] = total
 
-    conv(pad_g2, keep_back)
-    place_weights(0, False)
+    conv(pad_g2, 3, keep_back)
 
     own.wait()
     own_head.wait()
@@ -431,8 +463,12 @@
         pad_a1[h + 2, 0:cols] = act.astype(BF16)
 
     halo_a1 = halo_copies(pad_a1, 1)
-    halo_start(halo_a1)
+    halo_start(halo_a1, pad_a1, 1)
+    turn_act(pad_a1)
+    place_weights(0, True)
+    place_weights(1, False)
     halo_finish(halo_a1, pad_a1, 1)
+    turn_halo(pad_a1)
 
     def first_layer(h, total):
         x = (x_keep[h] + total).astype(BF16).astype(F32)
@@ -442,55 +478,63 @@
         g = cot_ref[h].astype(F32) + slope * back2[h]
         pad_g1[h + 2, 0:cols] = g.astype(BF16)
 
-    conv(pad_a1, first_layer)
+    conv(pad_a1, 0, first_layer)
     halo_a2 = halo_copies(pad_a2, 2)
-    halo_start(halo_a2)
+    halo_start(halo_a2, pad_a2, 2)
     halo_g1 = halo_copies(pad_g1, 3)
-    halo_start(halo_g1)
-
-    turn_act(pad_a1)
-    shift_grad(pad_g1)
+    halo_start(halo_g1, pad_g1, 3)
+
+    lat_plan = stage_plan(lat_parts, lon_parts, True)
+    lon_plan = stage_plan(lat_parts, lon_parts, False)
+    first_part = tile_count // (2 * parts) * parts
+    live = []
+
+    def start_sums(slot_of):
+        spans = [(0, first_part), (first_part, tile_count - first_part)]
+        for n, (start, length) in enumerate(spans):
+            if length:
+                steps = sum_steps(slot_of, start, length, 2 * slot_of + n, lon_plan if n == 0 else lat_plan)
+                next(steps)
+                live.append(steps)
+
+    def tick(count=1):
+        for _ in range(count):
+            if live:
+                steps = live.pop(0)
+                if next(steps, "end") != "end":
+                    live.append(steps)
+
+    shift_grad(pad_g1, 0)
     kernel_terms(pad_a1, 0)
-    sum_a = sum_steps(0, stage_plan(lat_parts, lon_parts, True))
-    next(sum_a)
-
+    start_sums(0)
+
+    turn_act(pad_a2)
     halo_finish(halo_a2, pad_a2, 2)
-    turn_act(pad_a2)
-    shift_grad(pad_g2)
-    next(sum_a, None)
-    kernel_terms(pad_a2, 1)
-    sum_b = sum_steps(1, stage_plan(lat_parts, lon_parts, False))
-    next(sum_b)
-    next(sum_a, None)
-
-    place_weights(0, True)
+    turn_halo(pad_a2)
+    tick(2)
+    kernel_terms(pad_a2, 1, tick)
+    start_sums(1)
     halo_finish(halo_g1, pad_g1, 3)
 
     def last_grad(h, total):
         g = pad_g1[h + 2, 0:cols].astype(F32) + slope1[h] * total
         back2[h] = g
 
-    conv(pad_g1, last_grad)
-    next(sum_b, None)
+    conv(pad_g1, 1, last_grad, lambda: tick(2))
     grads = jnp.dot(
         featx[...], back2[...].astype(BF16).reshape(rows * cols, channels), preferred_element_type=F32
     )
     small[0] = grads[0 : small.shape[1]].astype(BF16)
-    sum_c = small_steps(stage_plan(lat_parts, lon_parts, True))
+    sum_c = small_steps(lat_plan)
     next(sum_c)
-    next(sum_a, None)
-    next(sum_b, None)
-
-    place_weights(1, False)
+    live.insert(0, sum_c)
 
     def last_layer(h, total):
         enc_ref[h] = (x_keep[h] + total).astype(BF16)
 
-    conv(pad_a2, last_layer)
-
-    live = [sum_c, sum_a, sum_b]
+    conv(pad_a2, 2, last_layer, lambda: tick(3))
     while live:
-        live = [s for s in live if next(s, "end") != "end"]
+        tick()
 
     for copies in (halo_g2, halo_a1, halo_a2, halo_g1):
         halo_drain(copies)
@@ -499,6 +543,14 @@
     def _(dist):
         for copy in row_copies(dist):
             copy.wait_send()
+
+
+def widen(scale, enc_in, kgrad_in, small_in, enc_out, kgrad_out, obs_out, field_out):
+    enc_out[...] = enc_in[...]
+    kgrad_out[...] = scale * kgrad_in[...].astype(F32)
+    wide = scale * small_in[...].astype(F32)
+    obs_out[...] = wide[: obs_out.shape[0]]
+    field_out[...] = wide[obs_out.shape[0] : obs_out.shape[0] + field_out.shape[0]]
 
 
 def per_device(
@@ -536,14 +588,19 @@
             pltpu.VMEM((parts, 2, 128), F32),
             pltpu.VMEM((deep, rows * cols), BF16),
             pltpu.VMEM((deep, channels), BF16),
-            pltpu.VMEM((TAPS * channels, TAPS * channels), BF16),
+            pltpu.VMEM((4, TAPS * channels, TAPS * channels), BF16),
             *pads,
-            pltpu.VMEM((4, rows + 4, SIDE, channels), BF16),
-            pltpu.VMEM((4, rows + 4, SIDE, channels), BF16),
+            pltpu.VMEM((4, 4, SIDE, channels), BF16),
+            pltpu.VMEM((4, 4, SIDE, channels), BF16),
+            pltpu.VMEM((4, 2, 2, rows, channels), BF16),
+            pltpu.VMEM((4, 2, 2, rows, channels), BF16),
+            pltpu.VMEM((rows * SIDE, channels), F32),
+            pltpu.VMEM((rows * SIDE, channels), F32),
+            pltpu.VMEM((rows * SIDE, channels), F32),
+            pltpu.VMEM((fields * rows, cols), F32),
             pltpu.VMEM((rows + 4, channels, cols), BF16),
-            pltpu.VMEM((rows, cols, TAPS * channels), BF16),
-            pltpu.VMEM((rows, SIDE, TAPS * channels), BF16),
-            pltpu.VMEM((rows, cols, channels), F32),
+            pltpu.VMEM((2, rows, cols, TAPS * channels), BF16),
+            pltpu.VMEM((2, rows, SIDE, TAPS * channels), BF16),
             pltpu.VMEM((rows, cols, channels), F32),
             pltpu.VMEM((rows, cols, channels), F32),
             pltpu.VMEM((rows, cols, channels), F32),
@@ -558,10 +615,10 @@
             pltpu.SemaphoreType.DMA((2,)),
             pltpu.SemaphoreType.DMA((4, 8)),
             pltpu.SemaphoreType.DMA((4, 8)),
-            pltpu.SemaphoreType.DMA((2, hops)),
-            pltpu.SemaphoreType.DMA((2, hops)),
-            pltpu.SemaphoreType.DMA((2, hops)),
-            pltpu.SemaphoreType.DMA((2, hops)),
+            pltpu.SemaphoreType.DMA((4, hops)),
+            pltpu.SemaphoreType.DMA((4, hops)),
+            pltpu.SemaphoreType.DMA((4, hops)),
+            pltpu.SemaphoreType.DMA((4, hops)),
             pltpu.SemaphoreType.DMA((hops,)),
             pltpu.SemaphoreType.DMA((hops,)),
         ],
@@ -570,14 +627,36 @@
         ),
         name="encoder",
     )(
-        grid_fields.reshape(fields, rows * cols), obs_values, obs_count, obs_cell, obs_valid,
-        obs_dist2, field_weight, obs_weight, conv_kernel, cotangent,
+        grid_fields, obs_values, obs_count, jnp.swapaxes(obs_cell, 1, 2),
+        jnp.swapaxes(obs_valid, 1, 2), jnp.swapaxes(obs_dist2, 1, 2),
+        field_weight, obs_weight, conv_kernel, cotangent,
     )
     scale = 1.0 / (rows * lat_parts * cols * lon_parts) ** 0.5
     used = TAPS * TAPS * channels // 16
-    kernel_grad = scale * kgrad[:, :used].astype(F32).reshape(2, TAPS, TAPS, channels, channels)
-    small = scale * small.astype(F32)
-    return encoded, kernel_grad, small[:width], small[width : width + fields]
+    steps = math.gcd(math.gcd(used, rows), 4)
+    encoded, kernel_grad, obs_grad, field_grad = pl.pallas_call(
+        functools.partial(widen, scale),
+        grid=(steps,),
+        in_specs=[
+            pl.BlockSpec((rows // steps, cols, channels), lambda n: (n, 0, 0)),
+            pl.BlockSpec((2, used // steps, 16, channels), lambda n: (0, n, 0, 0)),
+            pl.BlockSpec((small_rows, channels), lambda n: (0, 0)),
+        ],
+        out_specs=[
+            pl.BlockSpec((rows // steps, cols, channels), lambda n: (n, 0, 0)),
+            pl.BlockSpec((2, used // steps, 16, channels), lambda n: (0, n, 0, 0)),
+            pl.BlockSpec((width, channels), lambda n: (0, 0)),
+            pl.BlockSpec((fields, channels), lambda n: (0, 0)),
+        ],
+        out_shape=(
+            jax.ShapeDtypeStruct((rows, cols, channels), BF16),
+            jax.ShapeDtypeStruct((2, used, 16, channels), F32),
+            jax.ShapeDtypeStruct((width, channels), F32),
+            jax.ShapeDtypeStruct((fields, channels), F32),
+        ),
+        name="widen",
+    )(encoded, kgrad, small)
+    return encoded, kernel_grad.reshape(2, TAPS, TAPS, channels, channels), obs_grad, field_grad
 
 
 def solution(mesh):

time: 102 us -> 86 us (0.84)
  local copies, waits for them, and re-layouts: 7.71 us -> 0 us
  Pallas kernels: 90 us -> 84.9 us
  other arithmetic: 3.47 us -> 0 us
    pallas_call x1, Pallas kernels: 90 us -> 80.8 us  [per_device(): pl.pallas_call(functools.partial(kernel, lat_parts, lon_parts), out_shape...]
    unnamed x9 -> x0, local copies, waits for them, and re-layouts: 6.48 us -> none
    pallas_call x0 -> x1, Pallas kernels: none -> 4.12 us  [per_device(): pl.pallas_call(functools.partial(widen, scale), grid=(steps,), in_specs=[...]
    mul x2 -> x0, other arithmetic: 3.47 us -> none  [the longest x1 3.46 us: per_device(): scale * kgrad[:, :used].astype(F32).reshape(2, TAPS, TAPS, channels, chan...]
    slice x2 -> x0, local copies, waits for them, and re-layouts: 1.24 us -> none  [per_device(): return (encoded, kernel_grad, small[:width], small[width:width + fields])]
where the time goes in v1:
time: 86 us; the launch traced here: 85.7 us
  Pallas kernels  84.9 us (99%)
    pallas_call x1, Pallas kernels, per_device(): pl.pallas_call(functools.partial(kernel, lat_parts, lon_parts), out_shape...  80.8 us
    pallas_call x1, Pallas kernels, per_device(): pl.pallas_call(functools.partial(widen, scale), grid=(steps,), in_specs=[...  4.12 us

profile of v1, /device:TPU:0, one launch (start us, length us, event | category | flops | bytes accessed | tf_op | source)
XLA Modules:
  0.0 85.7 jit_solution(6101474434475323727)
XLA Ops:
  0.6 80.8 %encoder.1 = (bf16[16,128,128]{2,1,0:T(8,128)(2,1)}, bf16[2,224,16,128]{3,2,1,0:T(8,128)(2,1)}, bf16[160,128]{1,0:T(8,128)(2,1)}) custom-call(bf16[24,16,128]{2,1,0:T(8,128)(2,1)} %fields_ref.1, bf16[1,32,16,128]{3,2,1,0:T(8,128)(2,1)} %values_ref.1, s32[1,32]{1,0:T(1,128)} %count_ref.1, s32[1,16,32]{2,1,0:T(8,128)} %bitcast.4, s32[1,16,32]{2,1,0:T(8,128)} %bitcast.5, ...), custom_call_target="tpu_custom_call" | custom-call | tf_op jit(solution)/shard_map/encoder/pallas_call | solution.py:576
  81.5 4.1 %widen.1 = (bf16[16,128,128]{2,1,0:T(8,128)(2,1)}, f32[2,200,16,128]{3,2,1,0:T(8,128)}, f32[128,128]{1,0:T(8,128)}, f32[24,128]{1,0:T(8,128)}) custom-call(bf16[16,128,128]{2,1,0:T(8,128)(2,1)} %get-tuple-element.11.enc_in, bf16[2,224,16,128]{3,2,1,0:T(8,128)(2,1)} %get-tuple-element.12.kgrad_in, bf16[160,128]{1,0:T(8,128)(2,1)} %get-tuple-element.13.small_in), custom_call_target="tpu_custom_call" | custom-call | tf_op jit(solution)/shard_map/widen/pallas_call | solution.py:637

commit v2 on v1

--- a/solution.py
+++ b/solution.py
@@ -210,22 +210,26 @@
                 between()
 
     def shift_grad(pad, at):
-        @pl.loop(0, rows)
-        def _(h):
-            ext = jnp.concatenate(
-                [pad[h + 2, 0:cols].astype(F32), jnp.zeros((SIDE, channels), F32)], axis=0
-            )
-            for q in range(TAPS):
-                shift = (q - 2) % wide
-                moved = (pltpu.roll(ext, shift, 0) if shift else ext).astype(BF16)
-                lanes = slice(q * channels, (q + 1) * channels)
-                shifted[at, h, :, lanes] = moved[:cols]
-                shifted_side[at, h, :, lanes] = moved[cols:]
+        @pl.loop(0, rows // group)
+        def _(b):
+            for r in range(group):
+                h = b * group + r
+                ext = jnp.concatenate(
+                    [pad[h + 2, 0:cols].astype(F32), jnp.zeros((SIDE, channels), F32)], axis=0
+                )
+                for q in range(TAPS):
+                    shift = (q - 2) % wide
+                    moved = (pltpu.roll(ext, shift, 0) if shift else ext).astype(BF16)
+                    lanes = slice(q * channels, (q + 1) * channels)
+                    shifted[at, h, :, lanes] = moved[:cols]
+                    shifted_side[at, h, :, lanes] = moved[cols:]
 
     def turn_act(pad):
-        @pl.loop(2, rows + 2)
-        def _(h):
-            turned[h] = pad[h, 0:cols].T
+        @pl.loop(0, rows // group)
+        def _(b):
+            for r in range(group):
+                h = b * group + r + 2
+                turned[h] = pad[h, 0:cols].T
 
     def turn_halo(pad):
         for h in (0, 1, rows + 2, rows + 3):
@@ -452,21 +456,21 @@
         dens = sums[width : width + 1]
         featx[0:width, pl.ds(start, block)] = (sums[0:width] / (1.0 + dens)).astype(BF16)
 
-    @pl.loop(0, rows)
-    def _(h):
-        start = pl.multiple_of(h * cols, cols)
-        feats = featx[:, pl.ds(start, cols)].T
+    @pl.loop(0, rows // group)
+    def _(b):
+        start = pl.multiple_of(b * group * cols, group * cols)
+        feats = featx[:, pl.ds(start, group * cols)].T
         x = jnp.dot(feats, wcat[...], preferred_element_type=F32).astype(BF16).astype(F32)
+        x = x.reshape(group, cols, channels)
         act, slope = gelu_pair(x)
-        x_keep[h] = x
-        slope1[h] = slope
-        pad_a1[h + 2, 0:cols] = act.astype(BF16)
+        at = pl.ds(b * group, group)
+        x_keep[at] = x
+        slope1[at] = slope
+        pad_a1[pl.ds(b * group + 2, group), 0:cols] = act.astype(BF16)
 
     halo_a1 = halo_copies(pad_a1, 1)
     halo_start(halo_a1, pad_a1, 1)
     turn_act(pad_a1)
-    place_weights(0, True)
-    place_weights(1, False)
     halo_finish(halo_a1, pad_a1, 1)
     turn_halo(pad_a1)
 
@@ -514,7 +518,9 @@
     tick(2)
     kernel_terms(pad_a2, 1, tick)
     start_sums(1)
+    place_weights(0, True)
     halo_finish(halo_g1, pad_g1, 3)
+    tick(2)
 
     def last_grad(h, total):
         g = pad_g1[h + 2, 0:cols].astype(F32) + slope1[h] * total
@@ -529,6 +535,8 @@
     next(sum_c)
     live.insert(0, sum_c)
 
+    place_weights(1, False)
+
     def last_layer(h, total):
         enc_ref[h] = (x_keep[h] + total).astype(BF16)
 
@@ -545,12 +553,20 @@
             copy.wait_send()
 
 
-def widen(scale, enc_in, kgrad_in, small_in, enc_out, kgrad_out, obs_out, field_out):
-    enc_out[...] = enc_in[...]
-    kgrad_out[...] = scale * kgrad_in[...].astype(F32)
+def widen(scale, chunks, enc_in, kgrad_in, small_in, enc_out, kgrad_out, obs_out, field_out, stage, sems):
+    copies = [pltpu.make_async_copy(enc_in, enc_out, sems.at[2 * chunks])]
+    copies[0].start()
+    per = stage.shape[1] // chunks
+    for n in range(2 * chunks):
+        at = (n // chunks, slice(n % chunks * per, (n % chunks + 1) * per))
+        stage[at] = scale * kgrad_in[at].astype(F32)
+        copies.append(pltpu.make_async_copy(stage.at[at], kgrad_out.at[at], sems.at[n]))
+        copies[-1].start()
     wide = scale * small_in[...].astype(F32)
     obs_out[...] = wide[: obs_out.shape[0]]
     field_out[...] = wide[obs_out.shape[0] : obs_out.shape[0] + field_out.shape[0]]
+    for copy in copies:
+        copy.wait()
 
 
 def per_device(
@@ -633,27 +649,22 @@
     )
     scale = 1.0 / (rows * lat_parts * cols * lon_parts) ** 0.5
     used = TAPS * TAPS * channels // 16
-    steps = math.gcd(math.gcd(used, rows), 4)
+    chunks = math.gcd(used, 4)
     encoded, kernel_grad, obs_grad, field_grad = pl.pallas_call(
-        functools.partial(widen, scale),
-        grid=(steps,),
-        in_specs=[
-            pl.BlockSpec((rows // steps, cols, channels), lambda n: (n, 0, 0)),
-            pl.BlockSpec((2, used // steps, 16, channels), lambda n: (0, n, 0, 0)),
-            pl.BlockSpec((small_rows, channels), lambda n: (0, 0)),
-        ],
-        out_specs=[
-            pl.BlockSpec((rows // steps, cols, channels), lambda n: (n, 0, 0)),
-            pl.BlockSpec((2, used // steps, 16, channels), lambda n: (0, n, 0, 0)),
-            pl.BlockSpec((width, channels), lambda n: (0, 0)),
-            pl.BlockSpec((fields, channels), lambda n: (0, 0)),
-        ],
+        functools.partial(widen, scale, chunks),
+        in_specs=[vmem] * 3,
+        out_specs=[pl.BlockSpec(memory_space=pl.ANY)] * 2 + [vmem] * 2,
         out_shape=(
             jax.ShapeDtypeStruct((rows, cols, channels), BF16),
             jax.ShapeDtypeStruct((2, used, 16, channels), F32),
             jax.ShapeDtypeStruct((width, channels), F32),
             jax.ShapeDtypeStruct((fields, channels), F32),
         ),
+        scratch_shapes=[
+            pltpu.VMEM((2, used, 16, channels), F32),
+            pltpu.SemaphoreType.DMA((2 * chunks + 1,)),
+        ],
+        compiler_params=pltpu.CompilerParams(vmem_limit_bytes=32 * 1024 * 1024),
         name="widen",
     )(encoded, kgrad, small)
     return encoded, kernel_grad.reshape(2, TAPS, TAPS, channels, channels), obs_grad, field_grad

time: 86 us -> 85.9 us (level)
  Pallas kernels: 84.9 us -> 81.5 us
  local copies, waits for them, and re-layouts: 0 us -> 3.31 us
    unnamed x0 -> x6, local copies, waits for them, and re-layouts: none -> 3.31 us
    pallas_call x1, Pallas kernels: 80.8 us -> 78.9 us  [per_device(): pl.pallas_call(functools.partial(kernel, lat_parts, lon_parts), out_shape...]
    pallas_call x1, Pallas kernels: 4.12 us -> 2.58 us  [per_device(): pl.pallas_call(functools.partial(widen, scale, chunks), in_specs=[vmem] *...]
where the time goes in v2:
time: 85.9 us; the launch traced here: 85.6 us
  Pallas kernels  81.5 us (95%)
  local copies, waits for them, and re-layouts  3.31 us (4%)
    pallas_call x1, Pallas kernels, per_device(): pl.pallas_call(functools.partial(kernel, lat_parts, lon_parts), out_shape...  78.9 us
    unnamed x6, local copies, waits for them, and re-layouts  3.31 us
    pallas_call x1, Pallas kernels, per_device(): pl.pallas_call(functools.partial(widen, scale, chunks), in_specs=[vmem] *...  2.58 us

profile of v2, /device:TPU:0, one launch (start us, length us, event | category | flops | bytes accessed | tf_op | source)
XLA Modules:
  0.0 85.6 jit_solution(5726662419598262660)
XLA Ops:
  0.6 78.9 %encoder.1 = (bf16[16,128,128]{2,1,0:T(8,128)(2,1)}, bf16[2,224,16,128]{3,2,1,0:T(8,128)(2,1)}, bf16[160,128]{1,0:T(8,128)(2,1)}) custom-call(bf16[24,16,128]{2,1,0:T(8,128)(2,1)} %fields_ref.1, bf16[1,32,16,128]{3,2,1,0:T(8,128)(2,1)} %values_ref.1, s32[1,32]{1,0:T(1,128)} %count_ref.1, s32[1,16,32]{2,1,0:T(8,128)} %bitcast.4, s32[1,16,32]{2,1,0:T(8,128)} %bitcast.5, ...), custom_call_target="tpu_custom_call" | custom-call | tf_op jit(solution)/shard_map/encoder/pallas_call | solution.py:592
  79.5 0.0 copy-start
  79.6 1.5 %copy-done = bf16[2,224,16,128]{3,2,1,0:T(8,128)(2,1)S(1)} copy-done((bf16[2,224,16,128]{3,2,1,0:T(8,128)(2,1)S(1)}, bf16[2,224,16,128]{3,2,1,0:T(8,128)(2,1)}, u32[]{:S(2)}) %copy-start) | copy-done | bytes 1835032
  81.0 0.0 copy-start.1
  81.0 1.0 %copy-done.1 = bf16[16,128,128]{2,1,0:T(8,128)(2,1)S(1)} copy-done((bf16[16,128,128]{2,1,0:T(8,128)(2,1)S(1)}, bf16[16,128,128]{2,1,0:T(8,128)(2,1)}, u32[]{:S(2)}) %copy-start.1) | copy-done | bytes 524312
  82.1 0.0 copy-start.2
  82.1 0.8 copy-done.2
  82.9 2.6 %widen.1 = (bf16[16,128,128]{2,1,0:T(8,128)(2,1)}, f32[2,200,16,128]{3,2,1,0:T(8,128)}, f32[128,128]{1,0:T(8,128)}, f32[24,128]{1,0:T(8,128)}) custom-call(bf16[16,128,128]{2,1,0:T(8,128)(2,1)S(1)} %copy-done.1, bf16[2,224,16,128]{3,2,1,0:T(8,128)(2,1)S(1)} %copy-done, bf16[160,128]{1,0:T(8,128)(2,1)S(1)} %copy-done.2), custom_call_target="tpu_custom_call" | custom-call | tf_op jit(solution)/shard_map/widen/pallas_call | solution.py:653
Async XLA Ops:
  79.5 1.5 %copy-start = (bf16[2,224,16,128]{3,2,1,0:T(8,128)(2,1)S(1)}, bf16[2,224,16,128]{3,2,1,0:T(8,128)(2,1)}, u32[]{:S(2)}) copy-start(bf16[2,224,16,128]{3,2,1,0:T(8,128)(2,1)} %get-tuple-element.12.kgrad_in) | copy-start | bytes 5505028
  81.0 1.0 %copy-start.1 = (bf16[16,128,128]{2,1,0:T(8,128)(2,1)S(1)}, bf16[16,128,128]{2,1,0:T(8,128)(2,1)}, u32[]{:S(2)}) copy-start(bf16[16,128,128]{2,1,0:T(8,128)(2,1)} %get-tuple-element.11.enc_in) | copy-start | bytes 1572868
  82.1 0.8 copy-start.2

commit v3 on v2

--- a/solution.py
+++ b/solution.py
@@ -55,11 +55,11 @@
     fields_ref, values_ref, count_ref, cell_ref, valid_ref, dist_ref,
     field_w_ref, obs_w_ref, conv_ref, cot_ref,
     enc_ref, kgrad_ref, small_ref,
-    header, vrecv, hrecv, featx, wcat, wbuf, pad_g2, pad_a1, pad_a2, pad_g1,
+    header, outgoing, arrived, enc_keep, featx, wcat, wbuf, pad_g2, pad_a1, pad_a2, pad_g1,
     left, right, strip_out, strip_in, strip_w, strip_e, strip_z, field_rows,
     turned, shifted, shifted_side, back2, x_keep, slope1,
     kacc, part, final, inbox, small, small_in,
-    a2a_send, a2a_recv, own_sem, halo_send, halo_recv,
+    a2a_send, a2a_recv, out_sem, halo_send, halo_recv,
     rs_send, rs_recv, ag_send, ag_recv, sm_send, sm_recv,
 ):
     lat = lax.axis_index("lat")
@@ -74,7 +74,7 @@
 
     def device_at(dist):
         peer = lax.rem(me + dist, parts)
-        return peer, (peer // lon_parts, lax.rem(peer, lon_parts))
+        return peer, (lax.div(peer, lon_parts), lax.rem(peer, lon_parts))
 
     barrier = pltpu.get_barrier_semaphore()
 
@@ -87,7 +87,16 @@
     weight = jnp.where(used, jnp.exp(-0.5 * dist_ref[0]), 0.0).astype(BF16).astype(F32)
     header[...] = jnp.zeros_like(header)
     header[:, 0, 0:capacity] = weight.T
-    header[:, 1, 0:capacity] = cell_ref[0].astype(F32).T
+    cells = cell_ref[0].astype(F32)
+    cell_row = jnp.floor(cells / cols)
+    header[:, 1, 0:capacity] = cell_row.T
+    header[:, 2, 0:capacity] = (cells - cell_row * cols).T
+    line = lax.broadcasted_iota(jnp.int32, (parts, 16, 128), 1)
+    head = jnp.zeros((parts, 16, 128), F32)
+    for n in range(3):
+        head = jnp.where(line == n, jnp.broadcast_to(header[:, n : n + 1, :], head.shape), head)
+    outgoing[:, 0:capacity] = values_ref[0]
+    outgoing[:, capacity:] = head.astype(BF16)
 
     def clear_edges(pad, k):
         zero = jnp.zeros((2, wide, channels), BF16)
@@ -272,6 +281,8 @@
             part[slot_of, used_tiles:] = jnp.zeros(
                 (tile_count - used_tiles, 16, channels), BF16
             )
+
+    leaving = []
 
     def sum_steps(slot_of, start, length, stream, plan):
         groups = [Group(stage, lat, lon) for stage in plan]
@@ -336,7 +347,11 @@
             base, length = low, length * g.size
         for copy in pending:
             copy.wait_send()
-        kgrad_ref[slot_of, whole] = final[slot_of, whole]
+        copy = pltpu.make_async_copy(
+            final.at[slot_of, whole], kgrad_ref.at[slot_of, whole], out_sem.at[stream]
+        )
+        copy.start()
+        leaving.append(copy)
 
     def small_steps(plan):
         nsem = 0
@@ -388,28 +403,16 @@
 
     pl.semaphore_wait(barrier, parts - 1)
 
-    own = pltpu.make_async_copy(values_ref.at[0, me], vrecv.at[me], own_sem.at[0])
-    own.start()
-    own_head = pltpu.make_async_copy(header.at[me], hrecv.at[me], own_sem.at[1])
-    own_head.start()
-
-    def row_copies(dist):
-        peer, dev = device_at(dist)
-        return [
-            pltpu.make_async_remote_copy(
-                src_ref=src, dst_ref=dst, send_sem=a2a_send.at[n, dist], recv_sem=a2a_recv.at[n, dist],
-                device_id=dev, device_id_type=MESH,
-            )
-            for n, (src, dst) in enumerate(
-                ((values_ref.at[0, peer], vrecv.at[me]), (header.at[peer], hrecv.at[me]))
-            )
-        ]
-
     @pl.loop(1, parts)
     def _(dist):
-        for copy in row_copies(dist):
-            copy.start()
-
+        peer, dev = device_at(dist)
+        pltpu.make_async_remote_copy(
+            src_ref=outgoing.at[peer], dst_ref=arrived.at[me],
+            send_sem=a2a_send.at[dist], recv_sem=a2a_recv.at[dist],
+            device_id=dev, device_id_type=MESH,
+        ).start()
+
+    arrived[me] = outgoing[me]
     halo_g2 = halo_copies(pad_g2, 0)
     halo_start(halo_g2, pad_g2, 0)
     shift_grad(pad_g2, 1)
@@ -421,29 +424,28 @@
 
     conv(pad_g2, 3, keep_back)
 
-    own.wait()
-    own_head.wait()
-
     @pl.loop(1, parts)
     def _(dist):
         sender = lax.rem(me + parts - dist, parts)
-        for n, dst in enumerate((vrecv.at[sender], hrecv.at[sender])):
-            pltpu.make_async_remote_copy(
-                src_ref=dst, dst_ref=dst, send_sem=a2a_send.at[n, dist], recv_sem=a2a_recv.at[n, dist],
-                device_id=device_at(dist)[1], device_id_type=MESH,
-            ).wait_recv()
+        pltpu.make_async_remote_copy(
+            src_ref=arrived.at[sender], dst_ref=arrived.at[sender],
+            send_sem=a2a_send.at[dist], recv_sem=a2a_recv.at[dist],
+            device_id=device_at(dist)[1], device_id_type=MESH,
+        ).wait_recv()
 
     count = parts * capacity
     lane = lax.broadcasted_iota(jnp.int32, (count, 128), 1)
     pick = lane == lax.rem(lax.broadcasted_iota(jnp.int32, (count, 128), 0), capacity)
 
+    head = arrived[:, capacity:].astype(F32)
+
     def column(n):
-        spread = jnp.broadcast_to(hrecv[:, n : n + 1, :], (parts, capacity, 128)).reshape(count, 128)
+        spread = jnp.broadcast_to(head[:, n : n + 1, :], (parts, capacity, 128)).reshape(count, 128)
         return jnp.sum(jnp.where(pick, spread, 0.0), axis=1, keepdims=True)
 
-    w_col, cell_col = column(0), column(1)
+    w_col, cell_col = column(0), column(1) * cols + column(2)
     values_t = jnp.concatenate(
-        [vrecv[...].reshape(count, width).T, jnp.ones((16, count), BF16)], axis=0
+        [arrived[:, 0:capacity].reshape(count, width).T, jnp.ones((16, count), BF16)], axis=0
     )
     block = 512 if (rows * cols) % 512 == 0 else cols
 
@@ -482,7 +484,7 @@
         g = cot_ref[h].astype(F32) + slope * back2[h]
         pad_g1[h + 2, 0:cols] = g.astype(BF16)
 
-    conv(pad_a1, 0, first_layer)
+    conv(pad_a1, 0, first_layer, lambda: None)
     halo_a2 = halo_copies(pad_a2, 2)
     halo_start(halo_a2, pad_a2, 2)
     halo_g1 = halo_copies(pad_g1, 3)
@@ -538,9 +540,12 @@
     place_weights(1, False)
 
     def last_layer(h, total):
-        enc_ref[h] = (x_keep[h] + total).astype(BF16)
+        enc_keep[h] = (x_keep[h] + total).astype(BF16)
 
     conv(pad_a2, 2, last_layer, lambda: tick(3))
+    copy = pltpu.make_async_copy(enc_keep, enc_ref, out_sem.at[4])
+    copy.start()
+    leaving.append(copy)
     while live:
         tick()
 
@@ -549,23 +554,43 @@
 
     @pl.loop(1, parts)
     def _(dist):
-        for copy in row_copies(dist):
-            copy.wait_send()
-
-
-def widen(scale, chunks, enc_in, kgrad_in, small_in, enc_out, kgrad_out, obs_out, field_out, stage, sems):
-    copies = [pltpu.make_async_copy(enc_in, enc_out, sems.at[2 * chunks])]
-    copies[0].start()
+        peer, dev = device_at(dist)
+        pltpu.make_async_remote_copy(
+            src_ref=outgoing.at[peer], dst_ref=arrived.at[me],
+            send_sem=a2a_send.at[dist], recv_sem=a2a_recv.at[dist],
+            device_id=dev, device_id_type=MESH,
+        ).wait_send()
+
+    for copy in leaving:
+        copy.wait()
+
+
+def widen(
+    scale, chunks, enc_in, kgrad_in, small_in, enc_out, kgrad_out, obs_out, field_out,
+    narrow, stage, enc_keep, in_sems, out_sems,
+):
     per = stage.shape[1] // chunks
-    for n in range(2 * chunks):
-        at = (n // chunks, slice(n % chunks * per, (n % chunks + 1) * per))
-        stage[at] = scale * kgrad_in[at].astype(F32)
-        copies.append(pltpu.make_async_copy(stage.at[at], kgrad_out.at[at], sems.at[n]))
-        copies[-1].start()
+    spans = [(n // chunks, slice(n % chunks * per, (n % chunks + 1) * per)) for n in range(2 * chunks)]
+    loads = [
+        pltpu.make_async_copy(kgrad_in.at[at], narrow.at[at], in_sems.at[n])
+        for n, at in enumerate(spans)
+    ]
+    loads.append(pltpu.make_async_copy(enc_in, enc_keep, in_sems.at[2 * chunks]))
+    for copy in loads:
+        copy.start()
+    stores = []
+    for n, at in enumerate(spans):
+        loads[n].wait()
+        stage[at] = scale * narrow[at].astype(F32)
+        stores.append(pltpu.make_async_copy(stage.at[at], kgrad_out.at[at], out_sems.at[n]))
+        stores[-1].start()
+    loads[-1].wait()
+    stores.append(pltpu.make_async_copy(enc_keep, enc_out, out_sems.at[2 * chunks]))
+    stores[-1].start()
     wide = scale * small_in[...].astype(F32)
     obs_out[...] = wide[: obs_out.shape[0]]
     field_out[...] = wide[obs_out.shape[0] : obs_out.shape[0] + field_out.shape[0]]
-    for copy in copies:
+    for copy in stores:
         copy.wait()
 
 
@@ -588,6 +613,7 @@
     deep = -(-(width + fields) // 128) * 128
     small_rows = -(-(width + fields) // 16) * 16
     vmem = pl.BlockSpec(memory_space=pltpu.VMEM)
+    anywhere = pl.BlockSpec(memory_space=pl.ANY)
     pads = [pltpu.VMEM((rows + 4, wide, channels), BF16)] * 4
     encoded, kgrad, small = pl.pallas_call(
         functools.partial(kernel, lat_parts, lon_parts),
@@ -597,11 +623,12 @@
             jax.ShapeDtypeStruct((small_rows, channels), BF16),
         ),
         in_specs=[vmem] * 10,
-        out_specs=(vmem, vmem, vmem),
+        out_specs=(anywhere, anywhere, vmem),
         scratch_shapes=[
-            pltpu.VMEM((parts, 2, 128), F32),
-            pltpu.VMEM((parts, capacity, width), BF16),
-            pltpu.VMEM((parts, 2, 128), F32),
+            pltpu.VMEM((parts, 3, 128), F32),
+            pltpu.VMEM((parts, capacity + 16, width), BF16),
+            pltpu.VMEM((parts, capacity + 16, width), BF16),
+            pltpu.VMEM((rows, cols, channels), BF16),
             pltpu.VMEM((deep, rows * cols), BF16),
             pltpu.VMEM((deep, channels), BF16),
             pltpu.VMEM((4, TAPS * channels, TAPS * channels), BF16),
@@ -626,9 +653,9 @@
             pltpu.VMEM((2, tiles, 16, channels), BF16),
             pltpu.VMEM((len(plan) + 1, small_rows, channels), BF16),
             pltpu.VMEM((hops, small_rows, channels), BF16),
-            pltpu.SemaphoreType.DMA((2, parts)),
-            pltpu.SemaphoreType.DMA((2, parts)),
-            pltpu.SemaphoreType.DMA((2,)),
+            pltpu.SemaphoreType.DMA((parts,)),
+            pltpu.SemaphoreType.DMA((parts,)),
+            pltpu.SemaphoreType.DMA((5,)),
             pltpu.SemaphoreType.DMA((4, 8)),
             pltpu.SemaphoreType.DMA((4, 8)),
             pltpu.SemaphoreType.DMA((4, hops)),
@@ -652,8 +679,8 @@
     chunks = math.gcd(used, 4)
     encoded, kernel_grad, obs_grad, field_grad = pl.pallas_call(
         functools.partial(widen, scale, chunks),
-        in_specs=[vmem] * 3,
-        out_specs=[pl.BlockSpec(memory_space=pl.ANY)] * 2 + [vmem] * 2,
+        in_specs=[anywhere] * 2 + [vmem],
+        out_specs=[anywhere] * 2 + [vmem] * 2,
         out_shape=(
             jax.ShapeDtypeStruct((rows, cols, channels), BF16),
             jax.ShapeDtypeStruct((2, used, 16, channels), F32),
@@ -661,10 +688,13 @@
             jax.ShapeDtypeStruct((fields, channels), F32),
         ),
         scratch_shapes=[
+            pltpu.VMEM((2, used, 16, channels), BF16),
             pltpu.VMEM((2, used, 16, channels), F32),
+            pltpu.VMEM((rows, cols, channels), BF16),
+            pltpu.SemaphoreType.DMA((2 * chunks + 1,)),
             pltpu.SemaphoreType.DMA((2 * chunks + 1,)),
         ],
-        compiler_params=pltpu.CompilerParams(vmem_limit_bytes=32 * 1024 * 1024),
+        compiler_params=pltpu.CompilerParams(vmem_limit_bytes=56 * 1024 * 1024),
         name="widen",
     )(encoded, kgrad, small)
     return encoded, kernel_grad.reshape(2, TAPS, TAPS, channels, channels), obs_grad, field_grad

time: 85.9 us -> 85.5 us (level)
  local copies, waits for them, and re-layouts: 3.31 us -> 0 us
  Pallas kernels: 81.5 us -> 84.5 us
    unnamed x6 -> x0, local copies, waits for them, and re-layouts: 3.31 us -> none
    pallas_call x1, Pallas kernels: 2.58 us -> 4.4 us  [per_device(): pl.pallas_call(functools.partial(widen, scale, chunks), in_specs=[anywher...]
    pallas_call x1, Pallas kernels: 78.9 us -> 80.1 us  [per_device(): pl.pallas_call(functools.partial(kernel, lat_parts, lon_parts), out_shape...]
where the time goes in v3:
time: 85.5 us; the launch traced here: 85.3 us
  Pallas kernels  84.5 us (99%)
    pallas_call x1, Pallas kernels, per_device(): pl.pallas_call(functools.partial(kernel, lat_parts, lon_parts), out_shape...  80.1 us
    pallas_call x1, Pallas kernels, per_device(): pl.pallas_call(functools.partial(widen, scale, chunks), in_specs=[anywher...  4.4 us

profile of v3, /device:TPU:0, one launch (start us, length us, event | category | flops | bytes accessed | tf_op | source)
XLA Modules:
  0.0 85.3 jit_solution(11154276739008944032)
XLA Ops:
  0.6 80.1 %encoder.1 = (bf16[16,128,128]{2,1,0:T(8,128)(2,1)}, bf16[2,224,16,128]{3,2,1,0:T(8,128)(2,1)}, bf16[160,128]{1,0:T(8,128)(2,1)}) custom-call(bf16[24,16,128]{2,1,0:T(8,128)(2,1)} %fields_ref.1, bf16[1,32,16,128]{3,2,1,0:T(8,128)(2,1)} %values_ref.1, s32[1,32]{1,0:T(1,128)} %count_ref.1, s32[1,16,32]{2,1,0:T(8,128)} %bitcast.4, s32[1,16,32]{2,1,0:T(8,128)} %bitcast.5, ...), custom_call_target="tpu_custom_call" | custom-call | tf_op jit(solution)/shard_map/encoder/pallas_call | solution.py:618
  80.7 4.4 %widen.1 = (bf16[16,128,128]{2,1,0:T(8,128)(2,1)}, f32[2,200,16,128]{3,2,1,0:T(8,128)}, f32[128,128]{1,0:T(8,128)}, f32[24,128]{1,0:T(8,128)}) custom-call(bf16[16,128,128]{2,1,0:T(8,128)(2,1)} %get-tuple-element.11.enc_in, bf16[2,224,16,128]{3,2,1,0:T(8,128)(2,1)} %get-tuple-element.12.kgrad_in, bf16[160,128]{1,0:T(8,128)(2,1)} %get-tuple-element.13.small_in), custom_call_target="tpu_custom_call" | custom-call | tf_op jit(solution)/shard_map/widen/pallas_call | solution.py:680

commit v4 on v3

--- a/solution.py
+++ b/solution.py
@@ -52,14 +52,14 @@
 
 def kernel(
     lat_parts, lon_parts,
-    fields_ref, values_ref, count_ref, cell_ref, valid_ref, dist_ref,
-    field_w_ref, obs_w_ref, conv_ref, cot_ref,
+    fields_ref, values_hbm, count_ref, cell_ref, valid_ref, dist_ref,
+    field_w_ref, obs_w_ref, conv_hbm, cot_hbm,
     enc_ref, kgrad_ref, small_ref,
-    header, outgoing, arrived, enc_keep, featx, wcat, wbuf, pad_g2, pad_a1, pad_a2, pad_g1,
+    conv_ref, cot_ref, header, outgoing, arrived, enc_keep, featx, wcat, wbuf, pad_g2, pad_a1, pad_a2, pad_g1,
     left, right, strip_out, strip_in, strip_w, strip_e, strip_z, field_rows,
     turned, shifted, shifted_side, back2, x_keep, slope1,
     kacc, part, final, inbox, small, small_in,
-    a2a_send, a2a_recv, out_sem, halo_send, halo_recv,
+    a2a_send, a2a_recv, in_sem, out_sem, halo_send, halo_recv,
     rs_send, rs_recv, ag_send, ag_recv, sm_send, sm_recv,
 ):
     lat = lax.axis_index("lat")
@@ -67,7 +67,7 @@
     parts = lat_parts * lon_parts
     me = lat * lon_parts + lon
     rows, cols, channels = cot_ref.shape
-    capacity = values_ref.shape[2]
+    capacity, width = values_hbm.shape[2:]
     side = slice(cols, cols + SIDE)
     wide = cols + SIDE
     tile_count = part.shape[1]
@@ -81,6 +81,16 @@
     @pl.loop(1, parts)
     def _(dist):
         pl.semaphore_signal(barrier, inc=1, device_id=device_at(dist)[1], device_id_type=MESH)
+
+    load_rows = pltpu.make_async_copy(
+        values_hbm.at[0], outgoing.at[:, pl.ds(0, capacity)], in_sem.at[0]
+    )
+    load_cot = pltpu.make_async_copy(cot_hbm, cot_ref, in_sem.at[1])
+    load_conv = [
+        pltpu.make_async_copy(conv_hbm.at[n], conv_ref.at[n], in_sem.at[2 + n]) for n in range(2)
+    ]
+    for copy in (load_rows, load_cot, load_conv[1], load_conv[0]):
+        copy.start()
 
     slot = lax.broadcasted_iota(jnp.int32, (capacity, parts), 0)
     used = (valid_ref[0] == 1) & (slot < count_ref[...])
@@ -95,7 +105,6 @@
     head = jnp.zeros((parts, 16, 128), F32)
     for n in range(3):
         head = jnp.where(line == n, jnp.broadcast_to(header[:, n : n + 1, :], head.shape), head)
-    outgoing[:, 0:capacity] = values_ref[0]
     outgoing[:, capacity:] = head.astype(BF16)
 
     def clear_edges(pad, k):
@@ -384,13 +393,12 @@
             copy.wait_send()
         small_ref[...] = small[len(plan)]
 
+    load_cot.wait()
     pad_g2[2 : rows + 2, 0:cols] = cot_ref[...]
     for k, pad in enumerate((pad_g2, pad_a1, pad_a2, pad_g1)):
         clear_edges(pad, k)
     strip_z[...] = jnp.zeros_like(strip_z)
-    place_weights(1, True)
     field_count = fields_ref.shape[0]
-    width = values_ref.shape[3]
     featx[width:, :] = jnp.zeros((featx.shape[0] - width, featx.shape[1]), BF16)
     field_rows[...] = fields_ref[...].astype(F32).reshape(field_count * rows, cols)
     for h in range(rows):
@@ -401,6 +409,10 @@
     wcat[0:width] = obs_w_ref[...]
     wcat[width : width + field_count] = field_w_ref[...]
 
+    load_conv[1].wait()
+    place_weights(1, True)
+    load_rows.wait()
+
     pl.semaphore_wait(barrier, parts - 1)
 
     @pl.loop(1, parts)
@@ -416,6 +428,7 @@
     halo_g2 = halo_copies(pad_g2, 0)
     halo_start(halo_g2, pad_g2, 0)
     shift_grad(pad_g2, 1)
+    load_conv[0].wait()
     place_weights(0, False)
     halo_finish(halo_g2, pad_g2, 0)
 
@@ -484,7 +497,7 @@
         g = cot_ref[h].astype(F32) + slope * back2[h]
         pad_g1[h + 2, 0:cols] = g.astype(BF16)
 
-    conv(pad_a1, 0, first_layer, lambda: None)
+    conv(pad_a1, 0, first_layer)
     halo_a2 = halo_copies(pad_a2, 2)
     halo_start(halo_a2, pad_a2, 2)
     halo_g1 = halo_copies(pad_g1, 3)
@@ -518,8 +531,9 @@
     halo_finish(halo_a2, pad_a2, 2)
     turn_halo(pad_a2)
     tick(2)
-    kernel_terms(pad_a2, 1, tick)
+    kernel_terms(pad_a2, 1)
     start_sums(1)
+    tick(2)
     place_weights(0, True)
     halo_finish(halo_g1, pad_g1, 3)
     tick(2)
@@ -576,10 +590,13 @@
         for n, at in enumerate(spans)
     ]
     loads.append(pltpu.make_async_copy(enc_in, enc_keep, in_sems.at[2 * chunks]))
-    for copy in loads:
+    ahead = 2
+    for copy in loads[:ahead]:
         copy.start()
     stores = []
     for n, at in enumerate(spans):
+        if n + ahead < len(loads):
+            loads[n + ahead].start()
         loads[n].wait()
         stage[at] = scale * narrow[at].astype(F32)
         stores.append(pltpu.make_async_copy(stage.at[at], kgrad_out.at[at], out_sems.at[n]))
@@ -622,9 +639,11 @@
             jax.ShapeDtypeStruct((2, tiles, 16, channels), BF16),
             jax.ShapeDtypeStruct((small_rows, channels), BF16),
         ),
-        in_specs=[vmem] * 10,
+        in_specs=[vmem, anywhere] + [vmem] * 6 + [anywhere] * 2,
         out_specs=(anywhere, anywhere, vmem),
         scratch_shapes=[
+            pltpu.VMEM(conv_kernel.shape, BF16),
+            pltpu.VMEM((rows, cols, channels), BF16),
             pltpu.VMEM((parts, 3, 128), F32),
             pltpu.VMEM((parts, capacity + 16, width), BF16),
             pltpu.VMEM((parts, capacity + 16, width), BF16),
@@ -655,6 +674,7 @@
             pltpu.VMEM((hops, small_rows, channels), BF16),
             pltpu.SemaphoreType.DMA((parts,)),
             pltpu.SemaphoreType.DMA((parts,)),
+            pltpu.SemaphoreType.DMA((4,)),
             pltpu.SemaphoreType.DMA((5,)),
             pltpu.SemaphoreType.DMA((4, 8)),
             pltpu.SemaphoreType.DMA((4, 8)),
@@ -676,7 +696,7 @@
     )
     scale = 1.0 / (rows * lat_parts * cols * lon_parts) ** 0.5
     used = TAPS * TAPS * channels // 16
-    chunks = math.gcd(used, 4)
+    chunks = math.gcd(used, 8)
     encoded, kernel_grad, obs_grad, field_grad = pl.pallas_call(
         functools.partial(widen, scale, chunks),
         in_specs=[anywhere] * 2 + [vmem],

time: 85.5 us -> 80.2 us (0.938)
  Pallas kernels: 84.5 us -> 79.1 us
    pallas_call x1, Pallas kernels: 80.1 us -> 70.5 us  [per_device(): pl.pallas_call(functools.partial(kernel, lat_parts, lon_parts), out_shape...]
    pallas_call x1, Pallas kernels: 4.4 us -> 8.65 us  [per_device(): pl.pallas_call(functools.partial(widen, scale, chunks), in_specs=[anywher...]
where the time goes in v4:
time: 80.2 us; the launch traced here: 79.7 us
  Pallas kernels  79.1 us (99%)
    pallas_call x1, Pallas kernels, per_device(): pl.pallas_call(functools.partial(kernel, lat_parts, lon_parts), out_shape...  70.5 us
    pallas_call x1, Pallas kernels, per_device(): pl.pallas_call(functools.partial(widen, scale, chunks), in_specs=[anywher...  8.65 us

profile of v4, /device:TPU:0, one launch (start us, length us, event | category | flops | bytes accessed | tf_op | source)
XLA Modules:
  0.0 79.7 jit_solution(8662687484010270671)
XLA Ops:
  0.6 70.5 %encoder.1 = (bf16[16,128,128]{2,1,0:T(8,128)(2,1)}, bf16[2,224,16,128]{3,2,1,0:T(8,128)(2,1)}, bf16[160,128]{1,0:T(8,128)(2,1)}) custom-call(bf16[24,16,128]{2,1,0:T(8,128)(2,1)} %fields_ref.1, bf16[1,32,16,128]{3,2,1,0:T(8,128)(2,1)} %values_hbm.1, s32[1,32]{1,0:T(1,128)} %count_ref.1, s32[1,16,32]{2,1,0:T(8,128)} %bitcast.4, s32[1,16,32]{2,1,0:T(8,128)} %bitcast.5, ...), custom_call_target="tpu_custom_call" | custom-call | tf_op jit(solution)/shard_map/encoder/pallas_call | solution.py:635
  71.1 8.6 %widen.1 = (bf16[16,128,128]{2,1,0:T(8,128)(2,1)}, f32[2,200,16,128]{3,2,1,0:T(8,128)}, f32[128,128]{1,0:T(8,128)}, f32[24,128]{1,0:T(8,128)}) custom-call(bf16[16,128,128]{2,1,0:T(8,128)(2,1)} %get-tuple-element.11.enc_in, bf16[2,224,16,128]{3,2,1,0:T(8,128)(2,1)} %get-tuple-element.12.kgrad_in, bf16[160,128]{1,0:T(8,128)(2,1)} %get-tuple-element.13.small_in), custom_call_target="tpu_custom_call" | custom-call | tf_op jit(solution)/shard_map/widen/pallas_call | solution.py:700
